TPU v7x, 32 devices: a whole 2x2x4 slice. The times are simulated.
32 devices in a mesh: groups: 2 (over y), freq: 4 (over z), read: 2 (over x), pair: 2 (over core).
Axes of the slice: x: 2, y: 2, z: 4, core: 2. Of those that a mesh axis runs over, the one named last changes fastest.
Arguments:
- exposures: float32 [8, 2048, 2048], P(('groups', 'read', 'pair'), 'freq'), parts along dimension 0, may hold values from -6 to 6
- stamps: float32 [8, 16, 16], P('groups'), parts along dimension 0, may hold values from -1 to 1, as said below
- zero_point: float32 [8], P('groups'), parts along dimension 0, may hold values from 0.5 to 2
- noise_var: float32 [8], P('groups'), parts along dimension 0, may hold values from 0.25 to 4
- footprint: int32 [8, 2], P('groups'), parts along dimension 0, may hold values from 0 to 2048, as said below
- accept: int32 [8], P('groups'), parts along dimension 0, may hold values from 0 to 1, as said below
- assign: int32 [8], P('groups'), parts along dimension 0, may hold values from 0 to 3, each once
Outputs:
- coadd: float32 [2, 4096, 1024], P(None, ('groups', 'read', 'pair'), 'freq'), parts along dimension 1
There are 2 independent parts, one for each index of `groups`. A program takes and returns all parts, laid end to end along the dimension named above; each array names one. Nothing has to cross between parts.
Inputs may be any that keep to these rules, and one draw needn't show every extreme that they name: `stamps`: each stamp is 1 at row 8 and column 8, and the absolute values of its other entries sum to at most 0.9. For every exposure footprint[e, 0] < footprint[e, 1] and the two differ by at least 512; some exposure covers all 2048 rows. `accept`: at least one exposure is rejected, and at least one exposure that covers all 2048 rows is accepted. `assign`: each exposure sits in exactly one slot.
All inputs are finite; a program needn't handle non-finite values.
Results may differ from a plain program's by a relative error of at most 0.0001.
Values sent between devices are 32-bit elements; how exact they have to be, the bound alone decides.
A program may use at most 64 MiB of HBM per device.

v0:
```python
import math
import jax
import jax.numpy as jnp
from jax import lax
from jax.sharding import PartitionSpec as P

HIGHEST = lax.Precision.HIGHEST
TWO_PI = 2.0 * math.pi
LANES = 128


def with_halo(block, sides, width):
    for axis, dim in sides:
        count = lax.axis_size(axis)
        forward = [(i, i + 1) for i in range(count - 1)]
        backward = [(target, source) for source, target in forward]
        low = lax.ppermute(
            lax.slice_in_dim(block, block.shape[dim] - width, None, axis=dim), axis, forward
        )
        high = lax.ppermute(lax.slice_in_dim(block, 0, width, axis=dim), axis, backward)
        block = jnp.concatenate([low, block, high], axis=dim)
    return block


def phase_table(left_ids, right_ids, modulus):
    product = left_ids[:, None] * right_ids[None, :] % modulus
    return product.astype(jnp.float32) * (TWO_PI / modulus)


def fourier(real_in, imag_in, length):
    outer = length // LANES
    lead = real_in.shape[:-1]
    outer_ids = jnp.arange(outer, dtype=jnp.int32)
    lane_ids = jnp.arange(LANES, dtype=jnp.int32)
    short_phase = phase_table(outer_ids, outer_ids, outer)
    cos_a = jnp.cos(short_phase)
    sin_a = jnp.sin(short_phase)
    shaped_re = real_in.reshape(lead + (outer, LANES))
    first_re = jnp.einsum("...ab,ad->...db", shaped_re, cos_a, precision=HIGHEST)
    first_im = -jnp.einsum("...ab,ad->...db", shaped_re, sin_a, precision=HIGHEST)
    if imag_in is not None:
        shaped_im = imag_in.reshape(lead + (outer, LANES))
        first_re = first_re + jnp.einsum("...ab,ad->...db", shaped_im, sin_a, precision=HIGHEST)
        first_im = first_im + jnp.einsum("...ab,ad->...db", shaped_im, cos_a, precision=HIGHEST)
    twist = phase_table(outer_ids, lane_ids, length)
    twist_cos = jnp.cos(twist)
    twist_sin = jnp.sin(twist)
    mid_re = first_re * twist_cos + first_im * twist_sin
    mid_im = first_im * twist_cos - first_re * twist_sin
    lane_phase = phase_table(lane_ids, lane_ids, LANES)
    cos_b = jnp.cos(lane_phase)
    sin_b = jnp.sin(lane_phase)
    out_re = jnp.einsum("...db,bc->...cd", mid_re, cos_b, precision=HIGHEST) + jnp.einsum(
        "...db,bc->...cd", mid_im, sin_b, precision=HIGHEST
    )
    out_im = jnp.einsum("...db,bc->...cd", mid_im, cos_b, precision=HIGHEST) - jnp.einsum(
        "...db,bc->...cd", mid_re, sin_b, precision=HIGHEST
    )
    return (out_re.reshape(lead + (length,)), out_im.reshape(lead + (length,)))


def pack_blocks(real_part, imag_part, blocks):
    lead = real_part.shape[:-1]
    slice_width = real_part.shape[-1] // blocks
    both = jnp.stack(
        [
            real_part.reshape(lead + (blocks, slice_width)),
            imag_part.reshape(lead + (blocks, slice_width)),
        ],
        axis=-2,
    )
    return both.reshape(lead + (blocks * 2 * slice_width,))


def stamp_columns(stamp_set, freq_ids, image_width):
    stamp_len = stamp_set.shape[1]
    offsets = jnp.arange(stamp_len, dtype=jnp.int32) - stamp_len // 2
    phases = phase_table(jnp.mod(offsets, image_width), freq_ids, image_width)
    q_real = jnp.einsum("nab,bp->nap", stamp_set, jnp.cos(phases), precision=HIGHEST)
    q_imag = -jnp.einsum("nab,bp->nap", stamp_set, jnp.sin(phases), precision=HIGHEST)
    return (q_real, q_imag)


def psf_spectrum(stamp_set, rows_u, freq_ids, image_height, image_width):
    stamp_len = stamp_set.shape[1]
    q_real, q_imag = stamp_columns(stamp_set, freq_ids, image_width)
    offsets = jnp.arange(stamp_len, dtype=jnp.int32) - stamp_len // 2
    phases = phase_table(rows_u, jnp.mod(offsets, image_height), image_height)
    cos_u = jnp.cos(phases)
    sin_u = jnp.sin(phases)
    p_real = jnp.einsum("ma,nap->nmp", cos_u, q_real, precision=HIGHEST) + jnp.einsum(
        "ma,nap->nmp", sin_u, q_imag, precision=HIGHEST
    )
    p_imag = jnp.einsum("ma,nap->nmp", cos_u, q_imag, precision=HIGHEST) - jnp.einsum(
        "ma,nap->nmp", sin_u, q_real, precision=HIGHEST
    )
    return (p_real, p_imag)


def per_device(exposures, stamps, zero_point, noise_var, footprint, accept, assign):
    exp_dev, rows_dev, image_width = exposures.shape
    freq_count = lax.axis_size("freq")
    reader_count = lax.axis_size(("read", "pair"))
    image_height = rows_dev * freq_count
    half_width = image_width // 2
    per_freq = half_width // freq_count
    out_rows = image_height // reader_count
    count_all = assign.shape[0]
    freq_at = lax.axis_index("freq")
    reader_at = lax.axis_index(("read", "pair"))
    labels = jnp.arange(count_all, dtype=jnp.int32)
    slot_ids = reader_at * exp_dev + jnp.arange(exp_dev, dtype=jnp.int32)
    owner_id = jnp.sum(jnp.where(slot_ids[:, None] == labels[None, :], assign[None, :], 0), axis=1)
    chosen = owner_id[:, None] == labels[None, :]
    low_row = jnp.sum(jnp.where(chosen, footprint[None, :, 0], 0), axis=1)
    high_row = jnp.sum(jnp.where(chosen, footprint[None, :, 1], 0), axis=1)
    accepted = accept.astype(jnp.float32)
    numer_weight = accepted * zero_point / noise_var
    denom_weight = accepted * zero_point * zero_point / noise_var
    local_weight = jnp.sum(jnp.where(chosen, numer_weight[None, :], 0.0), axis=1)
    local_stamps = jnp.sum(jnp.where(chosen[:, :, None, None], stamps[None], 0.0), axis=1)
    padded = with_halo(exposures, (("freq", 1),), 1)
    zero_col = jnp.zeros((exp_dev, rows_dev, 1), jnp.float32)
    left_cells = jnp.concatenate([zero_col, exposures[:, :, :-1]], axis=2)
    right_cells = jnp.concatenate([exposures[:, :, 1:], zero_col], axis=2)
    row_global = freq_at * rows_dev + jnp.arange(rows_dev, dtype=jnp.int32)
    inside = (row_global[None, :] >= low_row[:, None]) & (row_global[None, :] < high_row[:, None])
    beside = padded[:, :-2] + padded[:, 2:] + left_cells + right_cells
    cleaned = jnp.where(inside[:, :, None], exposures - 0.25 * beside, 0.0)
    rows_out = reader_at * out_rows + jnp.arange(out_rows, dtype=jnp.int32)
    cols_own = freq_at * per_freq + jnp.arange(per_freq, dtype=jnp.int32)
    all_real, all_imag = psf_spectrum(stamps, rows_out, cols_own, image_height, image_width)
    denom = jnp.einsum(
        "n,nmp->mp", denom_weight, all_real * all_real + all_imag * all_imag, precision=HIGHEST
    )
    spec_re, spec_im = fourier(cleaned, None, image_width)
    packed = pack_blocks(spec_re[:, :, :half_width], spec_im[:, :, :half_width], freq_count)
    spectra = jnp.transpose(packed, (1, 0, 2)).reshape(rows_dev, exp_dev, freq_count, 2 * per_freq)
    regrouped = lax.all_to_all(spectra, "freq", split_axis=2, concat_axis=0, tiled=True)
    regrouped = regrouped.reshape(image_height, exp_dev, 2, per_freq)
    col_re = jnp.transpose(regrouped[:, :, 0], (1, 2, 0))
    col_im = jnp.transpose(regrouped[:, :, 1], (1, 2, 0))
    grid_re, grid_im = fourier(col_re, col_im, image_height)
    rows_u = jnp.arange(out_rows * lax.axis_size(("read", "pair")), dtype=jnp.int32)
    kernel_real, kernel_imag = psf_spectrum(
        local_stamps, rows_u, cols_own, image_height, image_width
    )
    term_real = jnp.einsum(
        "e,emp,epm->mp", local_weight, kernel_real, grid_re, precision=HIGHEST
    ) + jnp.einsum("e,emp,epm->mp", local_weight, kernel_imag, grid_im, precision=HIGHEST)
    term_imag = jnp.einsum(
        "e,emp,epm->mp", local_weight, kernel_real, grid_im, precision=HIGHEST
    ) - jnp.einsum("e,emp,epm->mp", local_weight, kernel_imag, grid_re, precision=HIGHEST)
    summed = lax.psum_scatter(
        jnp.concatenate([term_real, term_imag], axis=1),
        ("read", "pair"),
        scatter_dimension=0,
        tiled=True,
    )
    numer_real = summed[:, :per_freq]
    numer_imag = summed[:, per_freq:]
    scale = 1.0 / math.sqrt(image_height * image_width)
    root = jnp.sqrt(denom)
    return jnp.stack([numer_real / root * scale, numer_imag / root * scale])


def solution(mesh):
    in_specs = (
        P(("groups", "read", "pair"), "freq", None),
        P("groups", None, None),
        P("groups"),
        P("groups"),
        P("groups", None),
        P("groups"),
        P("groups"),
    )
    out_specs = P(None, ("groups", "read", "pair"), "freq")
    return jax.shard_map(
        per_device, mesh=mesh, in_specs=in_specs, out_specs=out_specs, check_vma=False
    )
```

profile of v0, /device:TPU:0, one launch (start us, length us, event | category | flops | bytes accessed | tf_op | source)
XLA Modules:
  0.0 307.0 jit_solution(17262272560458219443)
XLA Ops:
  7.4 4.9 %collective-permute-start = (f32[1,1,2048]{2,1,0:T(1,128)S(1)}, f32[1,1,2048]{2,1,0:T(1,128)S(1)}, u32[]{:S(2)}, u32[]{:S(2)}) collective-permute-start(f32[1,1,2048]{2,1,0:T(1,128)S(1)} %get-tuple-element.17), channel_id=1, source_target_pairs={{0,4},{4,8},{8,12},{1,5},{5,9},{9,13},{2,6},{6,10},{10,14},{3,7},{... | collective-permute-start | bytes 24584 | tf_op jit(solution)/shard_map/ppermute | solution.py:17
  13.7 8.0 %fusion.260 = (f32[1,512,2047]{2,1,0:T(8,128)}, f32[1,512,2047]{2,1,0:T(8,128)}) fusion(f32[1,512,2048]{2,1,0:T(8,128)} %param.7), kind=kLoop, calls=%fused_computation.295 | loop fusion | bytes 16769024 | tf_op jit(solution)/shard_map/slice | solution.py:124
  22.4 1.3 fusion.152
  23.7 1.3 fusion.151
  25.1 9.1 %fusion.6 = f32[64,8,16,128]{3,1,2,0:T(8,128)S(1)} fusion(f32[1,512,2048]{2,1,0:T(8,128)} %param.7, f32[1,1,2048]{2,1,0:T(1,128)S(1)} %collective-permute-done.1, f32[1,1,2048]{2,1,0:T(1,128)S(1)} %collective-permute-done, f32[1,512,2047]{2,1,0:T(8,128)} %get-tuple-element.16, f32[1,512,2047]{2,1,0:T(8,128)} %get-tuple-element.15, pred[512]{0:T(512)(128)(4,1)S(1)} %fusion.151), kind=kLoop, calls=%fused_computation.7 | loop fusion | flops 8388608 | bytes 16790016
  35.1 4.0 %fusion.119 = f32[16,512,128]{2,0,1:T(8,128)S(1)} fusion(f32[512,16,128]{2,1,0:T(8,128)S(1)} %bitcast.210), kind=kOutput, calls=%fused_computation.151 | convolution fusion | flops 201330176 | bytes 8388608 | tf_op jit(solution)/shard_map/...ab,ad->...db/dot_general | solution.py:40
  39.1 4.8 %fusion.8 = (f32[512,16,128]{2,1,0:T(8,128)S(1)}, f32[512,16,128]{2,1,0:T(8,128)S(1)}) fusion(f32[16,512,128]{2,0,1:T(8,128)S(1)} %fusion.119, f32[16,128]{1,0:T(8,128)S(1)} %get-tuple-element.23, f32[16,128]{1,0:T(8,128)S(1)} %get-tuple-element.24, f32[512,16,128]{2,1,0:T(8,128)S(1)} %bitcast.211), kind=kOutput, calls=%fused_computation.14 | convolution fusion | flops 208670208 | bytes 16793600 | tf_op jit(solution)/shard_map/...ab,ad->...db/dot_general | solution.py:39
  44.0 5.9 %fusion.13 = f32[128,512,16]{1,0,2:T(8,128)S(1)} fusion(f32[512,16,128]{2,1,0:T(8,128)S(1)} %get-tuple-element.8), kind=kOutput, calls=%fused_computation.23 | convolution fusion | flops 1610842112 | bytes 8388608 | tf_op jit(solution)/shard_map/...db,bc->...cd/dot_general | solution.py:53
  49.9 5.4 %fusion.11 = f32[128,512,16]{1,0,2:T(8,128)S(1)} fusion(f32[512,16,128]{2,1,0:T(8,128)S(1)} %get-tuple-element.8), kind=kOutput, calls=%fused_computation.21 | convolution fusion | flops 1610842112 | bytes 8388608 | tf_op jit(solution)/shard_map/...db,bc->...cd/dot_general | solution.py:56
  55.3 6.2 %add_bitcast_fusion = f32[1,512,128,16]{1,2,3,0:T(8,128)S(1)} fusion(f32[128,512,16]{1,0,2:T(8,128)S(1)} %fusion.13, f32[512,16,128]{2,1,0:T(8,128)S(1)} %get-tuple-element.7), kind=kOutput, calls=%fused_computation.20 | convolution fusion | flops 1611890688 | bytes 12582912 | tf_op jit(solution)/shard_map/...db,bc->...cd/dot_general | solution.py:53
  61.5 2.4 copy.70
  64.1 5.9 %subtract_bitcast_fusion = f32[1,512,128,16]{1,2,3,0:T(8,128)S(1)} fusion(f32[128,512,16]{1,0,2:T(8,128)S(1)} %fusion.11, f32[512,16,128]{2,1,0:T(8,128)S(1)} %get-tuple-element.7), kind=kOutput, calls=%fused_computation.19 | convolution fusion | flops 1611890688 | bytes 12582912 | tf_op jit(solution)/shard_map/...db,bc->...cd/dot_general | solution.py:56
  70.0 2.6 copy.73
  73.3 2.7 copy.74
  76.0 6.1 %all-to-all-start = ((f32[512,1,4,512]{0,3,1,2:T(8,128)}), f32[512,1,4,512]{0,3,1,2:T(8,128)}, u32[]{:S(2)}, u32[]{:S(2)}) async-start(f32[512,1,4,512]{0,3,1,2:T(8,128)} %bitcast.212), calls=%async_computation | async-start | bytes 8388608 | tf_op jit(solution)/shard_map/all_to_all | solution.py:139
  82.9 1.3 multiply_divide_fusion
  84.8 5.7 %fusion.61 = f32[256,2048]{1,0:T(8,128)S(1)} fusion(f32[16,256]{1,0:T(8,128)S(1)} %fusion.129, s32[16]{0:T(128)S(1)} %and_select_fusion), kind=kOutput, calls=%fused_computation.88 | convolution fusion | flops 101122048 | bytes 2113600 | tf_op jit(solution)/shard_map/ma,nap->nmp/dot_general | solution.py:91
  90.5 7.2 %fusion.59 = f32[256,2048]{1,0:T(8,128)} fusion(f32[16,256]{1,0:T(8,128)S(1)} %convolution_negate_fusion.1, s32[16]{0:T(128)S(1)} %and_select_fusion), kind=kOutput, calls=%fused_computation.87 | convolution fusion | flops 101122048 | bytes 2113600 | tf_op jit(solution)/shard_map/ma,nap->nmp/dot_general | solution.py:94
  97.8 7.8 %fusion.22 = f32[2048,256]{0,1:T(8,128)} fusion(f32[256,2048]{1,0:T(8,128)S(1)} %fusion.61, f32[16,256]{1,0:T(8,128)S(1)} %convolution_negate_fusion.1, f32[]{:T(128)} %get-tuple-element.22, s32[16]{0:T(128)S(1)} %and_select_fusion), kind=kOutput, calls=%fused_computation.34 | convolution fusion | flops 102170624 | bytes 4210756 | tf_op jit(solution)/shard_map/ma,nap->nmp/dot_general | solution.py:91
  105.6 69.5 %all-to-all-done = f32[512,1,4,512]{0,3,1,2:T(8,128)} async-done(((f32[512,1,4,512]{0,3,1,2:T(8,128)}), f32[512,1,4,512]{0,3,1,2:T(8,128)}, u32[]{:S(2)}, u32[]{:S(2)}) %all-to-all-start) | async-done | bytes 4194336 | tf_op jit(solution)/shard_map/all_to_all | solution.py:139
  175.0 5.3 %copy.76 = f32[4,512,1,1,512]{4,1,0,3,2:T(8,128)} copy(f32[4,512,1,1,512]{1,4,0,3,2:T(8,128)} %bitcast.25) | data formatting | bytes 8388608 | tf_op jit(solution)/shard_map/all_to_all | solution.py:139
  180.3 5.9 %reshape.291 = f32[2048,1,2,256]{3,2,0,1:T(2,128)} reshape(f32[4,512,1,1,512]{4,1,0,3,2:T(8,128)} %copy.76) | data formatting | bytes 8388608 | tf_op jit(solution)/shard_map/reshape | solution.py:140
  186.2 7.6 %slice_bitcast_fusion = (f32[1,256,2048]{1,0,2:T(1,128)}, f32[1,256,2048]{1,0,2:T(1,128)S(1)}) fusion(f32[2048,1,2,256]{3,2,0,1:T(2,128)} %reshape.291), kind=kLoop, calls=%fused_computation.35 | loop fusion | bytes 8388608 | tf_op jit(solution)/shard_map/transpose | solution.py:142
  193.7 1.5 copy.93
  195.2 2.2 copy.91
  197.5 3.3 %fusion.116 = f32[16,256,128]{2,0,1:T(8,128)} fusion(f32[256,16,128]{2,1,0:T(8,128)S(1)} %copy.91), kind=kOutput, calls=%fused_computation.148 | convolution fusion | flops 100666880 | bytes 4194304 | tf_op jit(solution)/shard_map/...ab,ad->...db/dot_general | solution.py:40
  200.7 3.3 %fusion.122 = f32[16,256,128]{2,0,1:T(8,128)} fusion(f32[256,16,128]{2,1,0:T(8,128)S(1)} %copy.91), kind=kOutput, calls=%fused_computation.154 | convolution fusion | flops 100666880 | bytes 4194304 | tf_op jit(solution)/shard_map/...ab,ad->...db/dot_general | solution.py:39
  204.0 1.4 copy.94
  205.5 2.7 copy.92
  209.5 3.8 %negate_add_fusion = f32[16,256,128]{2,0,1:T(8,128)S(1)} fusion(f32[16,256,128]{2,0,1:T(8,128)} %fusion.116, f32[256,16,128]{2,1,0:T(8,128)S(1)} %copy.92), kind=kOutput, calls=%fused_computation.55 | convolution fusion | flops 101715456 | bytes 6291456 | tf_op jit(solution)/shard_map/...ab,ad->...db/dot_general | solution.py:44
  213.3 4.0 %fusion.31 = (f32[256,16,128]{2,1,0:T(8,128)S(1)}, f32[256,16,128]{2,1,0:T(8,128)S(1)}) fusion(f32[16,256,128]{2,0,1:T(8,128)S(1)} %negate_add_fusion, f32[16,128]{1,0:T(8,128)S(1)} %get-tuple-element.23, f32[16,128]{1,0:T(8,128)S(1)} %get-tuple-element.24, f32[16,256,128]{2,0,1:T(8,128)S(1)} %copy-done.2, f32[256,16,128]{2,1,0:T(8,128)} %copy-done), kind=kOutput, calls=%fused_computation.48 | convolution fusion | flops 104336896 | bytes 10502144 | tf_op jit(solution)/shard_map/...ab,ad->...db/dot_general | solution.py:43
  217.3 2.6 fusion.36
  219.9 3.9 %fusion.34 = f32[128,256,16]{1,0,2:T(8,128)} fusion(f32[256,16,128]{2,1,0:T(8,128)S(1)} %get-tuple-element.12), kind=kOutput, calls=%fused_computation.56 | convolution fusion | flops 805535744 | bytes 4194304 | tf_op jit(solution)/shard_map/...db,bc->...cd/dot_general | solution.py:56
  223.8 2.8 add_bitcast_fusion.1
  226.6 2.5 copy.81
  229.1 2.9 copy.82
  232.0 4.2 %subtract_bitcast_fusion.1 = f32[1,256,128,16]{1,2,3,0:T(8,128)S(1)} fusion(f32[128,256,16]{1,0,2:T(8,128)} %fusion.34, f32[256,16,128]{2,1,0:T(8,128)S(1)} %get-tuple-element.11), kind=kOutput, calls=%fused_computation.53 | convolution fusion | flops 806060032 | bytes 6291456 | tf_op jit(solution)/shard_map/...db,bc->...cd/dot_general | solution.py:56
  236.2 2.5 copy.85
  238.8 3.1 %copy.86 = f32[256,2048]{1,0:T(8,128)} copy(f32[256,2048]{0,1:T(8,128)} %bitcast.218) | data formatting | bytes 4194304 | tf_op jit(solution)/shard_map/reshape.71
  241.9 9.1 %fusion.28 = (f32[2048,256]{0,1:T(8,128)S(1)}, f32[2048,256]{0,1:T(8,128)S(1)}) fusion(f32[256,2048]{1,0:T(8,128)} %copy.86, f32[2048,256]{0,1:T(8,128)} %fusion.22, f32[256,2048]{1,0:T(8,128)S(1)} %copy-done.1, f32[256,2048]{1,0:T(8,128)} %fusion.59, f32[16,256]{1,0:T(8,128)S(1)} %fusion.129, s32[16]{0:T(128)S(1)} %and_select_fusion, f32[]{:T(128)} %get-tuple-element.22), kind=kOutput, calls=%fused_computation.41 | convolution fusion | flops 105316352 | bytes 12599364 | tf_op jit(solution)/shard_map/ma,nap->nmp/dot_general | solution.py:94
  250.9 2.4 pad_maximum_fusion.3
  254.1 2.0 fusion.83
  256.1 1.9 fusion.85
  258.0 2.0 fusion.87
  260.0 2.5 fusion.27
  262.5 34.6 %reduce-scatter.2.cloned.1.call-done = f32[512,512]{0,1:T(8,128)} async-done(((f32[2048,512]{0,1:T(8,128)}), f32[512,512]{0,1:T(8,128)}) %reduce-scatter.2.cloned.1.call-update) | async-done | bytes 1048592 | tf_op jit(solution)/shard_map/reduce_scatter | solution.py:154
  297.1 1.4 fusion.56
  298.6 1.3 copy.87
  (42 shorter events, 8.1 us)
Async XLA Ops:
  7.4 17.6 %collective-permute-start = (f32[1,1,2048]{2,1,0:T(1,128)S(1)}, f32[1,1,2048]{2,1,0:T(1,128)S(1)}, u32[]{:S(2)}, u32[]{:S(2)}) collective-permute-start(f32[1,1,2048]{2,1,0:T(1,128)S(1)} %get-tuple-element.17), channel_id=1, source_target_pairs={{0,4},{4,8},{8,12},{1,5},{5,9},{9,13},{2,6},{6,10},{10,14},{3,7},{... | collective-permute-start | bytes 24584 | tf_op jit(solution)/shard_map/ppermute | solution.py:17
  12.4 12.7 %collective-permute-start.1 = (f32[1,1,2048]{2,1,0:T(1,128)S(1)}, f32[1,1,2048]{2,1,0:T(1,128)S(1)}, u32[]{:S(2)}, u32[]{:S(2)}) collective-permute-start(f32[1,1,2048]{2,1,0:T(1,128)S(1)} %get-tuple-element.18), channel_id=1, source_target_pairs={{4,0},{8,4},{12,8},{5,1},{9,5},{13,9},{6,2},{10,6},{14,10},{7,3},{... | collective-permute-start | bytes 24584 | tf_op jit(solution)/shard_map/ppermute | solution.py:20
  13.7 8.1 %copy-start.9 = (s32[4]{0:T(128)S(1)}, s32[4]{0:T(128)}, u32[]{:S(2)}) copy-start(s32[4]{0:T(128)} %param.13) | copy-start | bytes 52
  13.7 8.7 %copy-start.5 = (s32[4,2]{0,1:T(2,128)S(1)}, s32[4,2]{0,1:T(2,128)}, u32[]{:S(2)}) copy-start(s32[4,2]{0,1:T(2,128)} %param.11) | copy-start | bytes 100
  76.0 6.8 %copy-start.4 = (f32[4,16,16]{2,1,0:T(8,128)S(1)}, f32[4,16,16]{2,1,0:T(8,128)}, u32[]{:S(2)}) copy-start(f32[4,16,16]{2,1,0:T(8,128)} %param.8) | copy-start | bytes 12292
  76.0 6.9 %copy-start.6 = (f32[4]{0:T(128)S(1)}, f32[4]{0:T(128)}, u32[]{:S(2)}) copy-start(f32[4]{0:T(128)} %param.10) | copy-start | bytes 52
  76.0 6.9 %copy-start.7 = (f32[4]{0:T(128)S(1)}, f32[4]{0:T(128)}, u32[]{:S(2)}) copy-start(f32[4]{0:T(128)} %param.9) | copy-start | bytes 52
  76.0 6.9 %copy-start.8 = (s32[4]{0:T(128)S(1)}, s32[4]{0:T(128)}, u32[]{:S(2)}) copy-start(s32[4]{0:T(128)} %param.12) | copy-start | bytes 52
  76.0 99.0 %all-to-all-start = ((f32[512,1,4,512]{0,3,1,2:T(8,128)}), f32[512,1,4,512]{0,3,1,2:T(8,128)}, u32[]{:S(2)}, u32[]{:S(2)}) async-start(f32[512,1,4,512]{0,3,1,2:T(8,128)} %bitcast.212), calls=%async_computation | async-start | bytes 8388608 | tf_op jit(solution)/shard_map/all_to_all | solution.py:139
  82.1 215.0 %reduce-scatter.2.cloned.1.call-start = ((), (), s32[]{:S(2)}) async-start(), calls=%async_computation.2 | async-start | bytes 5242880 | tf_op jit(solution)/shard_map/reduce_scatter | solution.py:154
  200.7 3.3 %copy-start.3 = (f32[1,256,2048]{1,0,2:T(1,128)S(1)}, f32[1,256,2048]{1,0,2:T(1,128)}, u32[]{:S(2)}) copy-start(f32[1,256,2048]{1,0,2:T(1,128)} %get-tuple-element.13) | copy-start | bytes 6291460
  208.1 1.3 copy-start
  209.5 3.8 %copy-start.2 = (f32[16,256,128]{2,0,1:T(8,128)S(1)}, f32[16,256,128]{2,0,1:T(8,128)}, u32[]{:S(2)}) copy-start(f32[16,256,128]{2,0,1:T(8,128)} %fusion.122) | copy-start | bytes 6291460
  238.8 3.1 %copy-start.1 = (f32[256,2048]{1,0:T(8,128)S(1)}, f32[256,2048]{1,0:T(8,128)}, u32[]{:S(2)}) copy-start(f32[256,2048]{1,0:T(8,128)} %copy.82) | copy-start | bytes 6291460
Sparse Core Ops, SparseCore 0:
  253.5 43.5 reduce-scatter.1
where the time goes:
time: 311 us; the launch traced here: 307 us
  waiting for transfers between devices  104 us (33%)
  matrix products  99.5 us (32%)
  local copies, waits for them, and re-layouts  58.1 us (19%)
  other arithmetic  19 us (6%)
  between operations  14 us (5%)
  starting transfers between devices  12.3 us (4%)
    all_to_all x1, waiting for transfers between devices, per_device(): lax.all_to_all(spectra, 'freq', split_axis=2, concat_axis=0, tiled=True)  69.5 us
    reduce_scatter x1, waiting for transfers between devices, per_device(): lax.psum_scatter(jnp.concatenate([term_real, term_imag], axis=1), ('read'...  34.6 us
    dot_general x2, matrix products, psf_spectrum(): jnp.einsum('ma,nap->nmp', sin_u, q_real, precision=HIGHEST)  11.6 us
    another operation x4, local copies, waits for them, and re-layouts  10.9 us
    dot_general x2, matrix products, fourier(): jnp.einsum('...db,bc->...cd', mid_re, sin_b, precision=HIGHEST)  10.1 us
    dot_general x2, matrix products, psf_spectrum(): jnp.einsum('ma,nap->nmp', sin_u, q_imag, precision=HIGHEST)  9.76 us
    dot_general x2, matrix products, fourier(): jnp.einsum('...db,bc->...cd', mid_im, cos_b, precision=HIGHEST)  9.33 us
    dot_general x2, matrix products, psf_spectrum(): jnp.einsum('ma,nap->nmp', cos_u, q_imag, precision=HIGHEST)  9.2 us
  transfers between devices with their start and end apart: 4, of which 2 were waited for; matrix products, arithmetic and copies ran while one was open for 14% of the time, Pallas kernels for 0%

commit v1 on v0

--- a/solution.py
+++ b/solution.py
@@ -1,3 +1,4 @@
+import functools
 import math
 import jax
 import jax.numpy as jnp
@@ -7,6 +8,43 @@
 HIGHEST = lax.Precision.HIGHEST
 TWO_PI = 2.0 * math.pi
 LANES = 128
+
+
+def handle_lanes(payload, dim_k, chunk):
+    arr_next = payload.shape
+    x_new = payload.reshape(
+        *arr_next[:dim_k], chunk, arr_next[dim_k] // chunk, *arr_next[dim_k + 1 :]
+    )
+    return jnp.moveaxis(x_new, dim_k, 0)
+
+
+def feed_grid(w_in, dim_no):
+    w_in = jnp.moveaxis(w_in, 0, dim_no)
+    u_next = w_in.shape
+    return w_in.reshape(
+        *u_next[:dim_no], u_next[dim_no] * u_next[dim_no + 1], *u_next[dim_no + 2 :]
+    )
+
+
+def remake_block(vals, which_axis, original, patch):
+    mixed_arr = jax.lax.psum(1, axis_name=which_axis)
+    formed, local_next = (mixed_arr, jax.lax.axis_index(which_axis))
+    frame_out = handle_lanes(vals, original, formed)
+    nodes = [frame_out[local_next]]
+    s = 1
+    while s < formed:
+        heard = frame_out[local_next ^ s]
+        nodes.append(
+            jax.lax.ppermute(
+                heard, axis_name=which_axis, perm=[(to_i, to_i ^ s) for to_i in range(formed)]
+            )
+        )
+        s = s + 1
+    frame_out = jnp.stack(nodes)[local_next ^ jnp.arange(formed)]
+    return feed_grid(frame_out, patch)
+
+
+do_stacks_all_now = functools.partial(remake_block, which_axis="freq", original=2, patch=0)
 
 
 def with_halo(block, sides, width):
@@ -136,7 +174,7 @@
     spec_re, spec_im = fourier(cleaned, None, image_width)
     packed = pack_blocks(spec_re[:, :, :half_width], spec_im[:, :, :half_width], freq_count)
     spectra = jnp.transpose(packed, (1, 0, 2)).reshape(rows_dev, exp_dev, freq_count, 2 * per_freq)
-    regrouped = lax.all_to_all(spectra, "freq", split_axis=2, concat_axis=0, tiled=True)
+    regrouped = do_stacks_all_now(spectra)
     regrouped = regrouped.reshape(image_height, exp_dev, 2, per_freq)
     col_re = jnp.transpose(regrouped[:, :, 0], (1, 2, 0))
     col_im = jnp.transpose(regrouped[:, :, 1], (1, 2, 0))

time: 311 us -> 317 us (1.019)
  local copies, waits for them, and re-layouts: 58.1 us -> 65.9 us
  other arithmetic: 19 us -> 23.4 us
  waiting for transfers between devices: 104 us -> 99.8 us
    all_to_all x1 -> x0, waiting for transfers between devices: 69.5 us -> none  [per_device(): lax.all_to_all(spectra, 'freq', split_axis=2, concat_axis=0, tiled=True)]
    ppermute x0 -> x3, waiting for transfers between devices: none -> 48.2 us  [remake_block(): jax.lax.ppermute(heard, axis_name=which_axis, perm=[(to_i, to_i ^ s) for...]
    reduce_scatter x1, waiting for transfers between devices: 34.6 us -> 51.6 us  [per_device(): lax.psum_scatter(jnp.concatenate([term_real, term_imag], axis=1), ('read'...]
    unnamed x23 -> x21, local copies, waits for them, and re-layouts: 5.2 us -> 14.3 us
    slice x0 -> x1, local copies, waits for them, and re-layouts: none -> 8.06 us  [per_device(): col_im = jnp.transpose(regrouped[:, :, 1], (1, 2, 0))]
    transpose x1 -> x0, local copies, waits for them, and re-layouts: 7.57 us -> none  [per_device(): col_im = jnp.transpose(regrouped[:, :, 1], (1, 2, 0))]
    all_to_all x1 -> x0, starting transfers between devices: 6.1 us -> none  [per_device(): lax.all_to_all(spectra, 'freq', split_axis=2, concat_axis=0, tiled=True)]
    reshape x1 -> x0, local copies, waits for them, and re-layouts: 5.88 us -> none  [per_device(): regrouped = regrouped.reshape(image_height, exp_dev, 2, per_freq)]
  transfers between devices with their start and end apart: 4 -> 6, of which waited for: 2 -> 3; matrix products, arithmetic and copies ran while one was open for 14% -> 16% of each run, Pallas kernels for 0% -> 0%
where the time goes in v1:
time: 317 us; the launch traced here: 313 us
  waiting for transfers between devices  99.8 us (31%)
  matrix products  98.6 us (31%)
  local copies, waits for them, and re-layouts  65.9 us (21%)
  other arithmetic  23.4 us (7%)
  between operations  14.1 us (4%)
  starting transfers between devices  11.5 us (4%)
    reduce_scatter x1, waiting for transfers between devices, per_device(): lax.psum_scatter(jnp.concatenate([term_real, term_imag], axis=1), ('read'...  51.6 us
    ppermute x3, waiting for transfers between devices, remake_block(): jax.lax.ppermute(heard, axis_name=which_axis, perm=[(to_i, to_i ^ s) for...  48.2 us
    unnamed x21, local copies, waits for them, and re-layouts  14.3 us
    dot_general x2, matrix products, psf_spectrum(): jnp.einsum('ma,nap->nmp', sin_u, q_real, precision=HIGHEST)  12.7 us
    another operation x7, local copies, waits for them, and re-layouts  12.1 us
    dot_general x2, matrix products, psf_spectrum(): jnp.einsum('ma,nap->nmp', sin_u, q_imag, precision=HIGHEST)  10.8 us
    dot_general x2, matrix products, fourier(): jnp.einsum('...db,bc->...cd', mid_re, sin_b, precision=HIGHEST)  10.1 us
    dot_general x2, matrix products, psf_spectrum(): jnp.einsum('ma,nap->nmp', cos_u, q_imag, precision=HIGHEST)  9.86 us
  transfers between devices with their start and end apart: 6, of which 3 were waited for; matrix products, arithmetic and copies ran while one was open for 16% of the time, Pallas kernels for 0%

profile of v1, /device:TPU:0, one launch (start us, length us, event | category | flops | bytes accessed | tf_op | source)
XLA Modules:
  0.0 313.3 jit_solution(13764863678785626536)
XLA Ops:
  7.4 4.9 %collective-permute-start = (f32[1,1,2048]{2,1,0:T(1,128)S(1)}, f32[1,1,2048]{2,1,0:T(1,128)S(1)}, u32[]{:S(2)}, u32[]{:S(2)}) collective-permute-start(f32[1,1,2048]{2,1,0:T(1,128)S(1)} %get-tuple-element.21), channel_id=1, source_target_pairs={{0,4},{4,8},{8,12},{1,5},{5,9},{9,13},{2,6},{6,10},{10,14},{3,7},{... | collective-permute-start | bytes 24584 | tf_op jit(solution)/shard_map/ppermute | solution.py:55
  13.7 8.0 %fusion.262 = (f32[1,512,2047]{2,1,0:T(8,128)}, f32[1,512,2047]{2,1,0:T(8,128)}) fusion(f32[1,512,2048]{2,1,0:T(8,128)} %param.7), kind=kLoop, calls=%fused_computation.303 | loop fusion | bytes 16769024 | tf_op jit(solution)/shard_map/slice | solution.py:162
  23.8 1.3 fusion.178
  27.8 9.1 %fusion.6 = f32[64,8,16,128]{3,1,2,0:T(8,128)S(1)} fusion(f32[1,512,2048]{2,1,0:T(8,128)} %param.7, f32[1,1,2048]{2,1,0:T(1,128)S(1)} %collective-permute-done.1, f32[1,1,2048]{2,1,0:T(1,128)S(1)} %collective-permute-done, f32[1,512,2047]{2,1,0:T(8,128)} %get-tuple-element.20, f32[1,512,2047]{2,1,0:T(8,128)} %get-tuple-element.19, pred[512]{0:T(512)(128)(4,1)S(1)} %fusion.151), kind=kLoop, calls=%fused_computation.8 | loop fusion | flops 8388608 | bytes 16790016
  37.9 4.0 %fusion.119 = f32[16,512,128]{2,0,1:T(8,128)S(1)} fusion(f32[512,16,128]{2,1,0:T(8,128)S(1)} %bitcast.218), kind=kOutput, calls=%fused_computation.151 | convolution fusion | flops 201330176 | bytes 8388608 | tf_op jit(solution)/shard_map/...ab,ad->...db/dot_general | solution.py:78
  41.9 4.8 %fusion.8 = (f32[512,16,128]{2,1,0:T(8,128)S(1)}, f32[512,16,128]{2,1,0:T(8,128)S(1)}) fusion(f32[16,512,128]{2,0,1:T(8,128)S(1)} %fusion.119, f32[16,128]{1,0:T(8,128)S(1)} %get-tuple-element.27, f32[16,128]{1,0:T(8,128)S(1)} %get-tuple-element.28, f32[512,16,128]{2,1,0:T(8,128)S(1)} %bitcast.219), kind=kOutput, calls=%fused_computation.16 | convolution fusion | flops 208670208 | bytes 16793600 | tf_op jit(solution)/shard_map/...ab,ad->...db/dot_general | solution.py:77
  46.8 5.9 %fusion.13 = f32[128,512,16]{1,0,2:T(8,128)S(1)} fusion(f32[512,16,128]{2,1,0:T(8,128)S(1)} %get-tuple-element.8), kind=kOutput, calls=%fused_computation.25 | convolution fusion | flops 1610842112 | bytes 8388608 | tf_op jit(solution)/shard_map/...db,bc->...cd/dot_general | solution.py:91
  52.7 5.4 %fusion.11 = f32[128,512,16]{1,0,2:T(8,128)S(1)} fusion(f32[512,16,128]{2,1,0:T(8,128)S(1)} %get-tuple-element.8), kind=kOutput, calls=%fused_computation.23 | convolution fusion | flops 1610842112 | bytes 8388608 | tf_op jit(solution)/shard_map/...db,bc->...cd/dot_general | solution.py:94
  58.1 6.2 %add_bitcast_fusion = f32[1,512,128,16]{1,2,3,0:T(8,128)S(1)} fusion(f32[128,512,16]{1,0,2:T(8,128)S(1)} %fusion.13, f32[512,16,128]{2,1,0:T(8,128)S(1)} %get-tuple-element.7), kind=kOutput, calls=%fused_computation.22 | convolution fusion | flops 1611890688 | bytes 12582912 | tf_op jit(solution)/shard_map/...db,bc->...cd/dot_general | solution.py:91
  64.3 2.4 copy.20
  66.9 5.9 %subtract_bitcast_fusion = f32[1,512,128,16]{1,2,3,0:T(8,128)S(1)} fusion(f32[128,512,16]{1,0,2:T(8,128)S(1)} %fusion.11, f32[512,16,128]{2,1,0:T(8,128)S(1)} %get-tuple-element.7), kind=kOutput, calls=%fused_computation.21 | convolution fusion | flops 1611890688 | bytes 12582912 | tf_op jit(solution)/shard_map/...db,bc->...cd/dot_general | solution.py:94
  72.8 2.6 copy.23
  76.1 1.5 constant_dynamic-slice_fusion.3
  77.6 2.6 copy.27
  80.2 2.6 collective-permute-start.2
  84.2 2.6 collective-permute-start.3
  87.2 5.7 %fusion.61 = f32[256,2048]{1,0:T(8,128)S(1)} fusion(f32[16,256]{1,0:T(8,128)S(1)} %fusion.129, s32[16]{0:T(128)S(1)} %and_select_fusion), kind=kOutput, calls=%fused_computation.88 | convolution fusion | flops 101122048 | bytes 2113600 | tf_op jit(solution)/shard_map/ma,nap->nmp/dot_general | solution.py:129
  92.8 7.0 %fusion.59 = f32[256,2048]{1,0:T(8,128)} fusion(f32[16,256]{1,0:T(8,128)S(1)} %convolution_negate_fusion.1, s32[16]{0:T(128)S(1)} %and_select_fusion), kind=kOutput, calls=%fused_computation.87 | convolution fusion | flops 101122048 | bytes 2113600 | tf_op jit(solution)/shard_map/ma,nap->nmp/dot_general | solution.py:132
  99.9 8.0 %fusion.22 = f32[2048,256]{0,1:T(8,128)} fusion(f32[256,2048]{1,0:T(8,128)S(1)} %fusion.61, f32[16,256]{1,0:T(8,128)S(1)} %convolution_negate_fusion.1, f32[]{:T(128)} %get-tuple-element.26, s32[16]{0:T(128)S(1)} %and_select_fusion), kind=kOutput, calls=%fused_computation.36 | convolution fusion | flops 102170624 | bytes 4210756 | tf_op jit(solution)/shard_map/ma,nap->nmp/dot_general | solution.py:129
  108.2 18.3 %collective-permute-done.2 = f32[512,1,1,512]{3,0,2,1:T(8,128)} collective-permute-done((f32[512,1,1,512]{3,0,2,1:T(8,128)}, f32[512,1,1,512]{3,0,2,1:T(8,128)}, u32[]{:S(2)}, u32[]{:S(2)}) %collective-permute-start.2) | collective-permute-done | bytes 1048608 | tf_op jit(solution)/shard_map/ppermute | solution.py:38
  126.5 29.9 %collective-permute-done.3 = f32[512,1,1,512]{3,0,2,1:T(8,128)} collective-permute-done((f32[512,1,1,512]{3,0,2,1:T(8,128)}, f32[512,1,1,512]{3,0,2,1:T(8,128)}, u32[]{:S(2)}, u32[]{:S(2)}) %collective-permute-start.3) | collective-permute-done | bytes 1048608 | tf_op jit(solution)/shard_map/ppermute | solution.py:38
  156.4 4.3 %maximum_bitcast_fusion = f32[4,512,512]{2,1,0:T(8,128)} fusion(f32[1,512,1,1,512]{4,1,0,3,2:T(8,128)} %bitcast.31, f32[1,512,1,1,512]{4,1,0,3,2:T(8,128)} %bitcast.29, f32[1,512,1,1,512]{4,1,0,3,2:T(8,128)} %bitcast.27, f32[1,512,1,1,512]{4,1,0,3,2:T(8,128)S(1)} %bitcast.233), kind=kLoop, calls=%fused_computation.11 | loop fusion | flops 3145728 | bytes 8388608 | tf_op jit(solution)/shard_map/stack | solution.py:43
  160.8 5.0 %gather_fusion = f32[4,512,512]{2,1,0:T(8,128)} fusion(f32[4,512,512]{2,1,0:T(8,128)} %maximum_bitcast_fusion, s32[1024]{0:T(1024)S(1)} %pad_clamp_fusion), kind=kCustom, calls=%fused_computation | custom fusion | bytes 8388624 | tf_op jit(solution)/shard_map/gather | solution.py:43
  165.7 5.9 %reshape_reshape.3 = f32[2048,1,2,256]{3,2,0,1:T(2,128)} reshape(f32[4,512,512]{2,1,0:T(8,128)} %gather_fusion) | data formatting | bytes 8388608 | tf_op jit(solution)/shard_map/reshape;reshape | solution.py:178
  171.6 8.1 %fusion.261 = (f32[2048,1,1,256]{3,2,0,1:T(1,128)}, f32[2048,1,1,256]{3,2,0,1:T(1,128)}) fusion(f32[2048,1,2,256]{3,2,0,1:T(2,128)} %reshape_reshape.3), kind=kLoop, calls=%fused_computation.302 | loop fusion | bytes 8388608 | tf_op jit(solution)/shard_map/slice | solution.py:180
  179.7 4.6 %copy.44 = f32[2048,1,1,256]{0,3,2,1:T(8,128)S(1)} copy(f32[2048,1,1,256]{3,2,0,1:T(1,128)} %get-tuple-element.14) | data formatting | bytes 4194304
  184.6 1.9 fusion.116
  186.6 3.3 %fusion.122 = f32[16,256,128]{2,0,1:T(8,128)} fusion(f32[256,16,128]{2,1,0:T(8,128)S(1)} %bitcast.223), kind=kOutput, calls=%fused_computation.154 | convolution fusion | flops 100666880 | bytes 4194304 | tf_op jit(solution)/shard_map/...ab,ad->...db/dot_general | solution.py:77
  189.9 6.4 %copy.45 = f32[2048,1,1,256]{0,3,2,1:T(8,128)} copy(f32[2048,1,1,256]{3,2,0,1:T(1,128)} %get-tuple-element.13) | data formatting | bytes 4194304
  196.3 2.0 copy.48
  198.3 2.1 negate_add_fusion
  200.4 2.5 fusion.31
  202.8 2.6 fusion.36
  205.4 3.9 %fusion.34 = f32[128,256,16]{1,0,2:T(8,128)} fusion(f32[256,16,128]{2,1,0:T(8,128)S(1)} %get-tuple-element.12), kind=kOutput, calls=%fused_computation.56 | convolution fusion | flops 805535744 | bytes 4194304 | tf_op jit(solution)/shard_map/...db,bc->...cd/dot_general | solution.py:94
  209.3 2.8 add_bitcast_fusion.1
  212.1 2.5 copy.34
  214.7 2.9 copy.35
  217.6 4.2 %subtract_bitcast_fusion.1 = f32[1,256,128,16]{1,2,3,0:T(8,128)S(1)} fusion(f32[128,256,16]{1,0,2:T(8,128)} %fusion.34, f32[256,16,128]{2,1,0:T(8,128)S(1)} %get-tuple-element.11), kind=kOutput, calls=%fused_computation.53 | convolution fusion | flops 806060032 | bytes 6291456 | tf_op jit(solution)/shard_map/...db,bc->...cd/dot_general | solution.py:94
  221.8 2.5 copy.38
  224.4 3.1 copy.39
  227.5 9.1 %fusion.28 = (f32[2048,256]{0,1:T(8,128)S(1)}, f32[2048,256]{0,1:T(8,128)S(1)}) fusion(f32[256,2048]{1,0:T(8,128)} %copy.39, f32[2048,256]{0,1:T(8,128)} %fusion.22, f32[256,2048]{1,0:T(8,128)S(1)} %copy-done, f32[256,2048]{1,0:T(8,128)} %fusion.59, f32[16,256]{1,0:T(8,128)S(1)} %fusion.129, s32[16]{0:T(128)S(1)} %and_select_fusion, f32[]{:T(128)} %get-tuple-element.26), kind=kOutput, calls=%fused_computation.41 | convolution fusion | flops 105316352 | bytes 12599364 | tf_op jit(solution)/shard_map/ma,nap->nmp/dot_general | solution.py:132
  236.5 2.4 pad_maximum_fusion.3
  239.7 2.8 fusion.69
  242.5 2.8 fusion.71
  245.4 2.8 fusion.73
  248.2 3.6 %fusion.27 = f32[512,256]{0,1:T(8,128)S(1)} fusion(f32[4,256,512]{2,1,0:T(8,128)S(1)} %fusion.71, f32[4,256,512]{2,1,0:T(8,128)S(1)} %fusion.73, f32[4,256,512]{2,1,0:T(8,128)S(1)} %fusion.69, f32[4,16,256]{2,1,0:T(8,128)S(1)} %convolution_bitcast_fusion, f32[4]{0:T(128)S(1)} %get-tuple-element.25, s32[16]{0:T(128)S(1)} %and_select_fusion, ...), kind=kOutput, calls=%fused_computation.38 | convolution fusion | flops 104316928 | bytes 6883408 | tf_op jit(solution)/shard_map/ma,nap->nmp/dot_general | solution.py:132
  251.8 51.6 %reduce-scatter.2.cloned.1.call-done = f32[512,512]{0,1:T(8,128)} async-done(((f32[2048,512]{0,1:T(8,128)}), f32[512,512]{0,1:T(8,128)}) %reduce-scatter.2.cloned.1.call-update) | async-done | bytes 1048592 | tf_op jit(solution)/shard_map/reduce_scatter | solution.py:192
  303.4 1.4 fusion.56
  (49 shorter events, 13.1 us)
Async XLA Ops:
  6.5 296.9 %reduce-scatter.2.cloned.1.call-start = ((), (), s32[]{:S(2)}) async-start(), calls=%async_computation.1 | async-start | bytes 5242880 | tf_op jit(solution)/shard_map/reduce_scatter | solution.py:192
  7.4 20.4 %collective-permute-start = (f32[1,1,2048]{2,1,0:T(1,128)S(1)}, f32[1,1,2048]{2,1,0:T(1,128)S(1)}, u32[]{:S(2)}, u32[]{:S(2)}) collective-permute-start(f32[1,1,2048]{2,1,0:T(1,128)S(1)} %get-tuple-element.21), channel_id=1, source_target_pairs={{0,4},{4,8},{8,12},{1,5},{5,9},{9,13},{2,6},{6,10},{10,14},{3,7},{... | collective-permute-start | bytes 24584 | tf_op jit(solution)/shard_map/ppermute | solution.py:55
  12.4 15.5 %collective-permute-start.1 = (f32[1,1,2048]{2,1,0:T(1,128)S(1)}, f32[1,1,2048]{2,1,0:T(1,128)S(1)}, u32[]{:S(2)}, u32[]{:S(2)}) collective-permute-start(f32[1,1,2048]{2,1,0:T(1,128)S(1)} %get-tuple-element.22), channel_id=1, source_target_pairs={{4,0},{8,4},{12,8},{5,1},{9,5},{13,9},{6,2},{10,6},{14,10},{7,3},{... | collective-permute-start | bytes 24584 | tf_op jit(solution)/shard_map/ppermute | solution.py:58
  13.7 8.2 %copy-start.7 = (s32[4]{0:T(128)S(1)}, s32[4]{0:T(128)}, u32[]{:S(2)}) copy-start(s32[4]{0:T(128)} %param.13) | copy-start | bytes 52
  13.7 9.4 %copy-start.2 = (f32[4,16,16]{2,1,0:T(8,128)S(1)}, f32[4,16,16]{2,1,0:T(8,128)}, u32[]{:S(2)}) copy-start(f32[4,16,16]{2,1,0:T(8,128)} %param.8) | copy-start | bytes 12292
  13.7 10.1 %copy-start.3 = (s32[4,2]{0,1:T(2,128)S(1)}, s32[4,2]{0,1:T(2,128)}, u32[]{:S(2)}) copy-start(s32[4,2]{0,1:T(2,128)} %param.11) | copy-start | bytes 100
  13.7 11.4 %copy-start.4 = (f32[4]{0:T(128)S(1)}, f32[4]{0:T(128)}, u32[]{:S(2)}) copy-start(f32[4]{0:T(128)} %param.10) | copy-start | bytes 52
  13.7 11.4 %copy-start.5 = (f32[4]{0:T(128)S(1)}, f32[4]{0:T(128)}, u32[]{:S(2)}) copy-start(f32[4]{0:T(128)} %param.9) | copy-start | bytes 52
  13.7 11.4 %copy-start.6 = (s32[4]{0:T(128)S(1)}, s32[4]{0:T(128)}, u32[]{:S(2)}) copy-start(s32[4]{0:T(128)} %param.12) | copy-start | bytes 52
  80.2 46.3 %collective-permute-start.2 = (f32[512,1,1,512]{3,0,2,1:T(8,128)}, f32[512,1,1,512]{3,0,2,1:T(8,128)}, u32[]{:S(2)}, u32[]{:S(2)}) collective-permute-start(f32[512,1,1,512]{3,0,2,1:T(8,128)} %bitcast.234), channel_id=1, source_target_pairs={{0,4},{4,0},{8,12},{12,8},{1,5},{5,1},{9,13},{13,9},{2,6},{6,2},{1... | collective-permute-start | bytes 3145736 | tf_op jit(solution)/shard_map/ppermute | solution.py:38
  84.2 72.3 %collective-permute-start.3 = (f32[512,1,1,512]{3,0,2,1:T(8,128)}, f32[512,1,1,512]{3,0,2,1:T(8,128)}, u32[]{:S(2)}, u32[]{:S(2)}) collective-permute-start(f32[512,1,1,512]{3,0,2,1:T(8,128)} %bitcast.235), channel_id=1, source_target_pairs={{0,8},{4,12},{8,0},{12,4},{1,9},{5,13},{9,1},{13,5},{2,10},{6,14},... | collective-permute-start | bytes 3145736 | tf_op jit(solution)/shard_map/ppermute | solution.py:38
  87.1 69.3 %collective-permute-start.4 = (f32[512,1,1,512]{3,0,2,1:T(8,128)S(1)}, f32[512,1,1,512]{3,0,2,1:T(8,128)}, u32[]{:S(2)}, u32[]{:S(2)}) collective-permute-start(f32[512,1,1,512]{3,0,2,1:T(8,128)S(1)} %bitcast.236), channel_id=1, source_target_pairs={{0,12},{4,8},{8,4},{12,0},{1,13},{5,9},{9,5},{13,1},{2,14},{6,10},... | collective-permute-start | bytes 3145736 | tf_op jit(solution)/shard_map/ppermute | solution.py:38
  198.3 2.1 copy-start.1
  224.4 3.1 copy-start
Sparse Core Ops, SparseCore 0:
  239.1 64.2 reduce-scatter.1
